TPU v7x, 256 devices: a whole 4x4x8 slice. The times are simulated.
256 devices in a mesh: ctx: 64 (over y, x_lo, z), tp: 4 (over x_hi, core).
Axes of the slice: x: 4 (x_hi: 2, x_lo: 2; x = x_hi * 2 + x_lo), y: 4, z: 8, core: 2. Of those that a mesh axis runs over, the one named last changes fastest.
Arguments:
- queries: bfloat16 [16384, 4096], P('ctx', 'tp'), may hold values from -8 to 8
- latent_keys: bfloat16 [512, 4096], P(('ctx', 'tp')), may hold values from -8 to 8
- latent_values: bfloat16 [512, 4096], P(('ctx', 'tp')), may hold values from -6 to 6
- gate_logit: float32 [], replicated, may hold values from 0.3 to 1.2
- last_frame: int32 [128], P('ctx'), may hold values from 0 to 7, as said below
- cotangent: bfloat16 [16384, 4096], P('ctx', 'tp'), may hold values from -6 to 6
Outputs:
- attended: bfloat16 [16384, 4096], P('ctx', 'tp')
- query_grad: bfloat16 [16384, 4096], P('ctx', 'tp')
- key_grad: float32 [512, 4096], P(('ctx', 'tp'))
- value_grad: float32 [512, 4096], P(('ctx', 'tp'))
Inputs may be any that keep to these rules, and one draw needn't show every extreme that they name: Non-decreasing along the document; text block b sees the frames 0 to last_frame[b].
All inputs are finite; a program needn't handle non-finite values.
Results may differ from a plain program's by a relative error of at most 0.015.
Values may be sent and summed in bfloat16 or wider, within the bound.
No kernel may reach another device: no remote copies, remote signals or barrier semaphores. Data moves between devices by JAX's collectives and lax.ppermute only.
A program may use at most 64 MiB of HBM per device.

v0:
```python
import jax
import jax.numpy as jnp
from jax import lax
from jax.sharding import PartitionSpec as P

DH = 128
LATF = 64
TBLK = 128
masked_fill = -1e30


def per_device(queries, latent_keys, latent_values, gate_logit, last_frame, cotangent):
    tok_rows, columns = queries.shape
    head_count = columns // DH
    keys_every, values_every = (
        lax.all_gather(latent_keys, ("ctx", "tp"), axis=0, tiled=True),
        lax.all_gather(latent_values, ("ctx", "tp"), axis=0, tiled=True),
    )
    offset = lax.axis_index("tp") * columns
    keys_mine = lax.dynamic_slice_in_dim(keys_every, offset, columns, 1)
    values_mine = lax.dynamic_slice_in_dim(values_every, offset, columns, 1)
    latent_count = keys_mine.shape[0]
    keys_heads = keys_mine.reshape(latent_count, head_count, DH)
    values_heads = values_mine.reshape(latent_count, head_count, DH)
    score_scale = 1.0 / DH**0.5
    gate_value = jnp.tanh(gate_logit)
    frame_index = jnp.arange(latent_count, dtype=jnp.int32) // LATF
    last_tok = jnp.repeat(last_frame, TBLK, total_repeat_length=tok_rows)
    block_rows = min(512, tok_rows)
    block_count = tok_rows // block_rows

    def advance(running, block_index):
        row_start = block_index * block_rows
        query_block = queries.reshape(block_rows, head_count, DH)
        last_block = lax.dynamic_slice_in_dim(last_tok, row_start, block_rows, 0)
        visible = frame_index[None, :] <= last_block[:, None]
        scores = (
            jnp.einsum("qhd,khd->hqk", query_block, keys_heads, preferred_element_type=jnp.float32)
            * score_scale
        )
        scores = jnp.where(visible[None], scores, masked_fill)
        maxima = jnp.max(scores, axis=-1, keepdims=True)
        expo = jnp.where(visible[None], jnp.exp(scores - maxima), 0.0)
        totals = jnp.sum(expo, axis=-1, keepdims=True)
        weights = expo / totals
        weights_low = weights.astype(jnp.bfloat16)
        context = jnp.einsum(
            "hqk,khd->qhd", weights_low, values_heads, preferred_element_type=jnp.float32
        )
        attended = (gate_value * context.reshape(block_rows, columns)).astype(jnp.bfloat16)
        gated_cot = (gate_value * cotangent.astype(jnp.float32)).astype(jnp.bfloat16)
        gated_heads = gated_cot.reshape(block_rows, head_count, DH)
        prob_grad = jnp.einsum(
            "qhd,khd->hqk", gated_heads, values_heads, preferred_element_type=jnp.float32
        )
        inner_sum = jnp.sum(weights * prob_grad, axis=-1, keepdims=True)
        score_grad = (weights * (prob_grad - inner_sum) * score_scale).astype(jnp.bfloat16)
        query_grad = jnp.einsum(
            "hqk,khd->qhd", score_grad, keys_heads, preferred_element_type=jnp.float32
        )
        key_part = jnp.einsum(
            "hqk,qhd->khd", score_grad, query_block, preferred_element_type=jnp.float32
        )
        value_part = jnp.einsum(
            "hqk,qhd->khd", weights_low, gated_heads, preferred_element_type=jnp.float32
        )
        query_low = query_grad.reshape(block_rows, columns).astype(jnp.bfloat16)
        return ((running[0] + key_part, running[1] + value_part), (attended, query_low))

    zeros_kv = jnp.zeros((latent_count, head_count, DH), jnp.float32)
    sums, outputs = lax.scan(
        advance, (zeros_kv, zeros_kv), jnp.arange(block_count, dtype=jnp.int32)
    )
    attended = outputs[0].reshape(tok_rows, columns)
    query_grad = outputs[1].reshape(tok_rows, columns)
    key_terms = sums[0].reshape(latent_count, columns)
    value_terms = sums[1].reshape(latent_count, columns)
    key_total, value_total = lax.psum((key_terms, value_terms), "ctx")
    portion = latent_count // lax.axis_size("ctx")
    first_row = lax.axis_index("ctx") * portion
    key_own = lax.dynamic_slice_in_dim(key_total, first_row, portion, 0)
    value_own = lax.dynamic_slice_in_dim(value_total, first_row, portion, 0)
    key_grad, value_grad = (
        lax.all_to_all(
            key_own.astype(jnp.bfloat16), "tp", split_axis=0, concat_axis=1, tiled=True
        ).astype(key_own.dtype),
        lax.all_to_all(
            value_own.astype(jnp.bfloat16), "tp", split_axis=0, concat_axis=1, tiled=True
        ).astype(value_own.dtype),
    )
    return (attended, query_grad, key_grad, value_grad)


def solution(mesh):
    placed = (
        P("ctx", "tp"),
        P(("ctx", "tp"), None),
        P(("ctx", "tp"), None),
        P(),
        P("ctx"),
        P("ctx", "tp"),
    )
    return jax.shard_map(
        per_device,
        mesh=mesh,
        in_specs=placed,
        out_specs=(P("ctx", "tp"), P("ctx", "tp"), P(("ctx", "tp"), None), P(("ctx", "tp"), None)),
        check_vma=False,
    )
```

profile of v0, /device:TPU:1, one launch (start us, length us, event | category | flops | bytes accessed | tf_op | source)
XLA Modules:
  0.0 1265.6 jit_solution(15816836092543142598)
XLA Ops:
  9.3 2.0 copy.89
  11.4 1.1 multiply_convert_fusion.1
  12.5 1.0 copy.90
  13.5 1.3 fusion.37
  14.9 1.3 compare_select_fusion.1
  16.3 410.5 %all-gather.7.cloned.1.call-done = bf16[256,2,4096]{2,1,0:T(2,128)(2,1)} async-done(((bf16[1,2,4096]{2,1,0:T(2,128)(2,1)}), bf16[256,2,4096]{2,1,0:T(2,128)(2,1)}) %all-gather.7.cloned.1.call-update) | async-done | bytes 4194320 | tf_op jit(solution)/shard_map/all_gather | solution.py:16
  426.8 7.2 reshape.212
  434.0 406.2 %all-gather.5.cloned.1.call-done = bf16[256,2,4096]{2,1,0:T(2,128)(2,1)} async-done(((bf16[1,2,4096]{2,1,0:T(2,128)(2,1)}), bf16[256,2,4096]{2,1,0:T(2,128)(2,1)}) %all-gather.5.cloned.1.call-update) | async-done | bytes 4194320 | tf_op jit(solution)/shard_map/all_gather | solution.py:17
  840.2 7.2 reshape.210
  847.4 1.7 constant_dynamic-slice_fusion
  850.3 4.2 fusion.39
  854.5 3.8 fusion.38
  858.3 3.6 fusion.17
  861.9 2.2 fusion.21
  864.1 8.6 fusion.7
  872.7 1.9 copy.75
  874.6 3.0 copy.78
  877.6 302.5 %all-reduce.2 = (bf16[512,1024]{1,0:T(8,128)(2,1)}, bf16[512,1024]{1,0:T(8,128)(2,1)}) all-reduce(f32[512,1024]{1,0:T(8,128)S(1)} %copy.75, f32[512,1024]{1,0:T(8,128)} %copy.78), channel_id=1, replica_groups=mesh['ctx'=64,'tp'=4] {'ctx'}, use_global_device_ids=true, to_apply=%region_3.4 | all-reduce | flops 1048576 | bytes 6291456 | tf_op jit(solution)/shard_map/psum | solution.py:78
  1181.4 58.1 %all-to-all-start = ((bf16[4,2,1024]{2,1,0:T(2,128)(2,1)}), bf16[4,2,1024]{2,1,0:T(2,128)(2,1)S(1)}, u32[]{:S(2)}, u32[]{:S(2)}) async-start(bf16[4,2,1024]{2,1,0:T(2,128)(2,1)} %all_to_all.20), calls=%async_computation | async-start | bytes 32768 | tf_op jit(solution)/shard_map/all_to_all | solution.py:84
  1240.9 3.3 all-to-all-done
  1244.2 4.0 all-to-all-start.1
  1248.1 7.4 fusion.18
  1255.5 1.0 copy.79
  1256.5 1.0 copy.80
  (30 shorter events, 6.7 us)
Async XLA Ops:
  7.2 419.6 %all-gather.7.cloned.1.call-start = ((), (), s32[]{:S(2)}) async-start(), calls=%async_computation.3 | async-start | bytes 4210688 | tf_op jit(solution)/shard_map/all_gather | solution.py:16
  7.9 832.3 %all-gather.5.cloned.1.call-start = ((), (), s32[]{:S(2)}) async-start(), calls=%async_computation.2 | async-start | bytes 4210688 | tf_op jit(solution)/shard_map/all_gather | solution.py:17
  850.3 8.0 copy-start.1
  850.3 4.2 copy-start.3
  858.3 3.6 copy-start
  858.3 3.6 copy-start.5
  874.6 373.5 %copy-start.2 = (bf16[512,1024]{0,1:T(8,128)(2,1)S(1)}, bf16[512,1024]{0,1:T(8,128)(2,1)}, u32[]{:S(2)}) copy-start(bf16[512,1024]{0,1:T(8,128)(2,1)} %copy-done.1) | copy-start | bytes 3145732
  1181.4 62.8 %all-to-all-start = ((bf16[4,2,1024]{2,1,0:T(2,128)(2,1)}), bf16[4,2,1024]{2,1,0:T(2,128)(2,1)S(1)}, u32[]{:S(2)}, u32[]{:S(2)}) async-start(bf16[4,2,1024]{2,1,0:T(2,128)(2,1)} %all_to_all.20), calls=%async_computation | async-start | bytes 32768 | tf_op jit(solution)/shard_map/all_to_all | solution.py:84
  1244.2 14.0 %all-to-all-start.1 = ((bf16[4,2,1024]{2,1,0:T(2,128)(2,1)}), bf16[4,2,1024]{2,1,0:T(2,128)(2,1)S(1)}, u32[]{:S(2)}, u32[]{:S(2)}) async-start(bf16[4,2,1024]{2,1,0:T(2,128)(2,1)} %all_to_all.22), calls=%async_computation.1 | async-start | bytes 32768 | tf_op jit(solution)/shard_map/all_to_all | solution.py:87
  1248.1 7.4 copy-start.4
Sparse Core Ops, SparseCore 0:
  9.9 416.8 all-gather.6
  428.7 411.5 all-gather.4
where the time goes:
time: 1270 us
  waiting for transfers between devices  821 us (65%)
  blocking collectives  302 us (24%)
  starting transfers between devices  62.1 us (5%)
  local copies, waits for them, and re-layouts  31.2 us (2%)
  matrix products  29.7 us (2%)
  between operations  14.8 us (1%)
    all_gather x1, waiting for transfers between devices, per_device(): lax.all_gather(latent_keys, ('ctx', 'tp'), axis=0, tiled=True)  410 us
    all_gather x1, waiting for transfers between devices, per_device(): lax.all_gather(latent_values, ('ctx', 'tp'), axis=0, tiled=True)  406 us
    psum x1, blocking collectives, per_device(): key_total, value_total = lax.psum((key_terms, value_terms), 'ctx')  302 us
    all_to_all x1, starting transfers between devices, per_device(): lax.all_to_all(key_own.astype(jnp.bfloat16), 'tp', split_axis=0, concat_a...  58.1 us
  transfers between devices with their start and end apart: 4, of which 3 were waited for; matrix products, arithmetic and copies ran while one was open for 2% of the time, Pallas kernels for 0%

commit v1 on v0

--- a/solution.py
+++ b/solution.py
@@ -7,6 +7,16 @@
 LATF = 64
 TBLK = 128
 masked_fill = -1e30
+
+
+def show_ports(slab_in):
+    front = jnp.concatenate(
+        jax.lax.all_to_all(
+            jnp.stack(jnp.split(slab_in, jax.lax.axis_size("tp"), axis=0)), "tp", 0, 0
+        ),
+        axis=1,
+    )
+    return front
 
 
 def per_device(queries, latent_keys, latent_values, gate_logit, last_frame, cotangent):
@@ -81,9 +91,7 @@
     key_own = lax.dynamic_slice_in_dim(key_total, first_row, portion, 0)
     value_own = lax.dynamic_slice_in_dim(value_total, first_row, portion, 0)
     key_grad, value_grad = (
-        lax.all_to_all(
-            key_own.astype(jnp.bfloat16), "tp", split_axis=0, concat_axis=1, tiled=True
-        ).astype(key_own.dtype),
+        show_ports(key_own.astype(jnp.bfloat16)).astype(key_own.dtype),
         lax.all_to_all(
             value_own.astype(jnp.bfloat16), "tp", split_axis=0, concat_axis=1, tiled=True
         ).astype(value_own.dtype),

time: 1270 us -> 1270 us (level)
  no operation moved by 1% of the time
where the time goes in v1:
time: 1270 us
  waiting for transfers between devices  821 us (65%)
  blocking collectives  302 us (24%)
  starting transfers between devices  62.1 us (5%)
  local copies, waits for them, and re-layouts  30.6 us (2%)
  matrix products  29.7 us (2%)
  between operations  14.8 us (1%)
    all_gather x1, waiting for transfers between devices, per_device(): lax.all_gather(latent_keys, ('ctx', 'tp'), axis=0, tiled=True)  410 us
    all_gather x1, waiting for transfers between devices, per_device(): lax.all_gather(latent_values, ('ctx', 'tp'), axis=0, tiled=True)  406 us
    psum x1, blocking collectives, per_device(): key_total, value_total = lax.psum((key_terms, value_terms), 'ctx')  302 us
    all_to_all x1, starting transfers between devices, show_ports(): jax.lax.all_to_all(jnp.stack(jnp.split(slab_in, jax.lax.axis_size('tp'),...  58.1 us
  transfers between devices with their start and end apart: 4, of which 3 were waited for; matrix products, arithmetic and copies ran while one was open for 2% of the time, Pallas kernels for 0%

profile of v1, /device:TPU:1, one launch (start us, length us, event | category | flops | bytes accessed | tf_op | source)
XLA Modules:
  0.0 1265.7 jit_solution(13012332923227250353)
XLA Ops:
  9.3 2.0 copy.200
  11.4 1.1 multiply_convert_fusion.1
  12.5 1.0 copy.201
  13.5 1.3 fusion.37
  14.9 1.3 compare_select_fusion.1
  16.3 410.5 %all-gather.7.cloned.1.call-done = bf16[256,2,4096]{2,1,0:T(2,128)(2,1)} async-done(((bf16[1,2,4096]{2,1,0:T(2,128)(2,1)}), bf16[256,2,4096]{2,1,0:T(2,128)(2,1)}) %all-gather.7.cloned.1.call-update) | async-done | bytes 4194320 | tf_op jit(solution)/shard_map/all_gather | solution.py:26
  426.8 7.2 reshape.211
  434.0 406.2 %all-gather.5.cloned.1.call-done = bf16[256,2,4096]{2,1,0:T(2,128)(2,1)} async-done(((bf16[1,2,4096]{2,1,0:T(2,128)(2,1)}), bf16[256,2,4096]{2,1,0:T(2,128)(2,1)}) %all-gather.5.cloned.1.call-update) | async-done | bytes 4194320 | tf_op jit(solution)/shard_map/all_gather | solution.py:27
  840.2 7.2 reshape.209
  847.5 1.7 constant_dynamic-slice_fusion
  850.3 4.2 fusion.39
  854.5 3.8 fusion.38
  858.3 3.6 fusion.17
  861.9 2.2 fusion.21
  864.1 8.6 fusion.7
  872.7 1.9 copy.186
  874.6 3.0 copy.189
  877.7 302.5 %all-reduce.2 = (bf16[512,1024]{1,0:T(8,128)(2,1)}, bf16[512,1024]{1,0:T(8,128)(2,1)}) all-reduce(f32[512,1024]{1,0:T(8,128)S(1)} %copy.186, f32[512,1024]{1,0:T(8,128)} %copy.189), channel_id=1, replica_groups=mesh['ctx'=64,'tp'=4] {'ctx'}, use_global_device_ids=true, to_apply=%region_3.4 | all-reduce | flops 1048576 | bytes 6291456 | tf_op jit(solution)/shard_map/psum | solution.py:88
  1181.5 58.1 %all-to-all-start = ((bf16[4,2,1024]{2,1,0:T(2,128)(2,1)}), bf16[4,2,1024]{2,1,0:T(2,128)(2,1)S(1)}, u32[]{:S(2)}, u32[]{:S(2)}) async-start(bf16[4,2,1024]{2,1,0:T(2,128)(2,1)} %pad_maximum_fusion), calls=%async_computation | async-start | bytes 32768 | tf_op jit(solution)/shard_map/all_to_all | solution.py:14
  1240.9 3.3 all-to-all-done
  1244.2 3.9 all-to-all-start.1
  1248.2 7.4 fusion.18
  1255.6 1.0 copy.190
  1256.6 1.0 copy.191
  (31 shorter events, 6.7 us)
Async XLA Ops:
  7.2 419.6 %all-gather.7.cloned.1.call-start = ((), (), s32[]{:S(2)}) async-start(), calls=%async_computation.3 | async-start | bytes 4210688 | tf_op jit(solution)/shard_map/all_gather | solution.py:26
  7.9 832.3 %all-gather.5.cloned.1.call-start = ((), (), s32[]{:S(2)}) async-start(), calls=%async_computation.2 | async-start | bytes 4210688 | tf_op jit(solution)/shard_map/all_gather | solution.py:27
  850.3 8.0 copy-start.1
  850.3 4.2 copy-start.3
  858.3 3.6 copy-start
  858.3 3.6 copy-start.5
  874.6 373.6 %copy-start.2 = (bf16[512,1024]{0,1:T(8,128)(2,1)S(1)}, bf16[512,1024]{0,1:T(8,128)(2,1)}, u32[]{:S(2)}) copy-start(bf16[512,1024]{0,1:T(8,128)(2,1)} %copy-done.1) | copy-start | bytes 3145732
  1181.5 62.8 %all-to-all-start = ((bf16[4,2,1024]{2,1,0:T(2,128)(2,1)}), bf16[4,2,1024]{2,1,0:T(2,128)(2,1)S(1)}, u32[]{:S(2)}, u32[]{:S(2)}) async-start(bf16[4,2,1024]{2,1,0:T(2,128)(2,1)} %pad_maximum_fusion), calls=%async_computation | async-start | bytes 32768 | tf_op jit(solution)/shard_map/all_to_all | solution.py:14
  1244.2 14.0 %all-to-all-start.1 = ((bf16[4,2,1024]{2,1,0:T(2,128)(2,1)}), bf16[4,2,1024]{2,1,0:T(2,128)(2,1)S(1)}, u32[]{:S(2)}, u32[]{:S(2)}) async-start(bf16[4,2,1024]{2,1,0:T(2,128)(2,1)} %all_to_all.14), calls=%async_computation.1 | async-start | bytes 32768 | tf_op jit(solution)/shard_map/all_to_all | solution.py:95
  1248.2 7.4 copy-start.4
Sparse Core Ops, SparseCore 0:
  9.9 416.8 all-gather.6
  428.7 411.5 all-gather.4
